TPU v7x, 32 devices: a whole 2x2x4 slice. The times are simulated.
32 devices in a mesh: groups: 2 (over x), lblk: 16 (over z, y, core).
Axes of the slice: x: 2, y: 2, z: 4, core: 2. Of those that a mesh axis runs over, the one named last changes fastest.
Arguments:
- tables: bfloat16 [16, 4, 6144, 128], P('lblk'), may hold values from 0 to 0.00048828125
- spectra: bfloat16 [32, 4, 165, 128], P(('groups', 'lblk')), parts along dimension 0, may hold values from 0.099609375 to 10
- pairs: int32 [1024, 2], P(('groups', 'lblk')), parts along dimension 0, may hold values from 0 to 16, as said below
Outputs:
- coupling: float32 [32, 165, 6144], P(('groups', 'lblk')), parts along dimension 0
There are 2 independent parts, one for each index of `groups`. A program takes and returns all parts, laid end to end along the dimension named above; an argument that names none is the same for every part. Nothing has to cross between parts.
Inputs may be any that keep to these rules, and one draw needn't show every extreme that they name: Each slot holds a block id and a span id below 4; a block id of 16 marks an empty slot, whose span is 0. The pairs of one reader's list are distinct, and one reader lists at most 2 spans for one block; in every draw some block is listed with 2 spans by every reader.
All inputs are finite; a program needn't handle non-finite values.
Results may differ from a plain program's by a relative error of at most 0.0003.
Values may be sent and summed in bfloat16 or wider, within the bound.
A program may use at most 128 MiB of HBM per device.

v0:
```python
import jax
import jax.numpy as jnp
from jax import lax
from jax.sharding import PartitionSpec as P


def local(tables, spectra, pairs):
    owners = lax.axis_size("lblk")
    nchunk = tables.shape[1]
    block_ids = jnp.arange(owners, dtype=jnp.int32)
    span_ids = jnp.arange(nchunk, dtype=jnp.int32)
    block_match = (pairs[:, 0][:, None] == block_ids[None, :]).astype(jnp.bfloat16)
    span_match = (pairs[:, 1][:, None] == span_ids[None, :]).astype(jnp.bfloat16)
    needed = jnp.dot(block_match.T, span_match, preferred_element_type=jnp.float32)
    owner = lax.axis_index("lblk")
    flags = needed.astype(jnp.bfloat16)[None]
    reader_part = lax.all_gather(spectra, "lblk", axis=0, tiled=True)
    reader_flags = lax.all_gather(flags, "lblk", axis=0, tiled=True)
    column = lax.dynamic_index_in_dim(reader_flags, owner, 1, keepdims=False)
    mixed = jnp.einsum("rc,rcjk->cjk", column, reader_part, preferred_element_type=jnp.float32)
    coupling = jnp.einsum(
        "cjk,cik->ji", mixed, tables[0].astype(jnp.float32), precision=lax.Precision.HIGHEST
    )[None]
    return coupling


def solution(mesh):
    return jax.shard_map(
        local,
        mesh=mesh,
        in_specs=(
            P("lblk", None, None, None),
            P(("groups", "lblk"), None, None, None),
            P(("groups", "lblk"), None),
        ),
        out_specs=P(("groups", "lblk"), None, None),
        check_vma=False,
    )
```

profile of v0, /device:TPU:0, one launch (start us, length us, event | category | flops | bytes accessed | tf_op | source)
XLA Modules:
  0.0 79.6 jit_solution(10763692673668549966)
XLA Ops:
  6.5 0.0 all-gather.4.cloned.1.call-start
  6.5 0.7 all-gather.4.cloned.1.call-update
  7.3 0.8 slice_bitcast_fusion.1
  8.0 0.3 fusion.3
  8.3 23.1 %all-gather.1 = bf16[16,16,4]{1,2,0:T(4,128)(2,1)S(1)} all-gather(bf16[1,16,4]{1,2,0:T(4,128)(2,1)S(1)} %fusion.3), channel_id=2, replica_groups=mesh['groups'=2,'lblk'=16] {'lblk'}, dimensions={0}, use_global_device_ids=true | all-gather | bytes 2176 | tf_op jit(solution)/shard_map/all_gather | solution.py:18
  31.4 0.1 constant_dynamic-slice_fusion
  31.4 0.1 copy.6
  31.6 24.3 %all-gather.4.cloned.1.call-done = bf16[16,4,165,128]{3,1,2,0:T(4,128)(2,1)} async-done(((bf16[1,4,165,128]{3,1,2,0:T(4,128)(2,1)}), bf16[16,4,165,128]{3,1,2,0:T(4,128)(2,1)}) %all-gather.4.cloned.1.call-update) | async-done | bytes 2703376 | tf_op jit(solution)/shard_map/all_gather | solution.py:17
  55.8 2.3 %fusion.1 = f32[4,1,165,128]{3,1,2,0:T(1,128)S(1)} fusion(bf16[16,4,165,128]{3,1,2,0:T(4,128)(2,1)} %all-gather.4.cloned.1.call-done, bf16[16,4,1,1]{0,1,2,3:T(4,128)(2,1)S(1)} %bitcast.18), kind=kOutput, calls=%fused_computation.2 | convolution fusion | flops 2703360 | bytes 3041408 | tf_op jit(solution)/shard_map/rc,rcjk->cjk/dot_general | solution.py:20
  58.1 8.5 %convolution_bitcast_fusion = f32[1,165,6144]{2,1,0:T(8,128)S(1)} fusion(bf16[1,4,6144,128]{3,2,1,0:T(8,128)(2,1)} %param.3, f32[4,1,165,128]{3,1,2,0:T(1,128)S(1)} %fusion.1), kind=kOutput, calls=%fused_computation | convolution fusion | flops 6228541440 | bytes 10684416 | tf_op jit(solution)/shard_map/cjk,cik->ji/dot_general | solution.py:21
  66.6 6.1 %copy.7 = f32[1,165,6144]{2,0,1:T(1,128)} copy(f32[1,165,6144]{2,1,0:T(8,128)S(1)} %convolution_bitcast_fusion) | data formatting | bytes 8110080 | tf_op jit(solution)/shard_map/broadcast_in_dim | solution.py:21
Async XLA Ops:
  6.5 49.3 %all-gather.4.cloned.1.call-start = ((), (), s32[]{:S(2)}) async-start(), calls=%async_computation | async-start | bytes 2872320 | tf_op jit(solution)/shard_map/all_gather | solution.py:17
Sparse Core Ops, SparseCore 0:
  9.5 46.2 all-gather.3
where the time goes:
time: 79.7 us; the launch traced here: 79.6 us
  waiting for transfers between devices  25 us (31%)
  blocking collectives  23.1 us (29%)
  between operations  13.4 us (17%)
  matrix products  11 us (14%)
  local copies, waits for them, and re-layouts  7.09 us (9%)
    all_gather x1, waiting for transfers between devices, local(): reader_part = lax.all_gather(spectra, 'lblk', axis=0, tiled=True)  24.3 us
    all_gather x1, blocking collectives, local(): reader_flags = lax.all_gather(flags, 'lblk', axis=0, tiled=True)  23.1 us
    dot_general x1, matrix products, local(): jnp.einsum('cjk,cik->ji', mixed, tables[0].astype(jnp.float32), precision...  8.48 us
    broadcast_in_dim x1, local copies, waits for them, and re-layouts, local(): jnp.einsum('cjk,cik->ji', mixed, tables[0].astype(jnp.float32), precision...  6.13 us
    dot_general x1, matrix products, local(): jnp.einsum('rc,rcjk->cjk', column, reader_part, preferred_element_type=jn...  2.28 us
  transfers between devices with their start and end apart: 1, of which 1 were waited for; matrix products, arithmetic and copies ran while one was open for 2% of the time, Pallas kernels for 0%

commit v1 on v0

v1 whole, which is shorter than its diff:
```python
import functools

import jax
import jax.numpy as jnp
from jax import lax
from jax.experimental import pallas as pl
from jax.experimental.pallas import tpu as pltpu
from jax.sharding import PartitionSpec as P

LANES = 128
CORES = 2
TILE = 1024


def chip_grid(owners):
    chips = owners // CORES
    inner = 1
    while (inner * 2) ** 2 <= chips:
        inner *= 2
    return chips // inner, inner


def kernel(
    owners, lines, peers, cols,
    tables_ref, spectra_ref, pairs_ref, out_ref,
    raw, table_buf, sums, arrived, factors, own_sum,
    table_sem, up_send, up_recv, down_send, down_recv, core_send, core_recv, peer_send, peer_recv,
):
    spans = spectra_ref.shape[1]
    rows = raw.shape[3]
    me = lax.axis_index("lblk")
    line = me // (peers * CORES)
    row = (me // CORES) % peers
    core = me % CORES
    sibling = 1 - core

    def device(at_line, at_row, at_core):
        return {"lblk": (at_line * peers + at_row) * CORES + at_core}

    def up_copy(dist, span):
        slot = raw.at[jnp.maximum(line - dist, 0), core, span]
        return pltpu.make_async_remote_copy(
            src_ref=slot, dst_ref=slot, send_sem=up_send.at[dist, span], recv_sem=up_recv.at[dist, span],
            device_id=device(jnp.minimum(line + 1, lines - 1), row, core), device_id_type=pl.DeviceIdType.MESH)

    def down_copy(dist, span):
        slot = raw.at[jnp.minimum(line + dist, lines - 1), core, span]
        return pltpu.make_async_remote_copy(
            src_ref=slot, dst_ref=slot, send_sem=down_send.at[dist, span], recv_sem=down_recv.at[dist, span],
            device_id=device(jnp.maximum(line - 1, 0), row, core), device_id_type=pl.DeviceIdType.MESH)

    def core_copy(at_line, span):
        slot = raw.at[at_line, core, span]
        return pltpu.make_async_remote_copy(
            src_ref=slot, dst_ref=slot, send_sem=core_send.at[at_line, span], recv_sem=core_recv.at[at_line, span],
            device_id=device(line, row, sibling), device_id_type=pl.DeviceIdType.MESH)

    def peer_copy(step, span):
        return pltpu.make_async_remote_copy(
            src_ref=sums.at[step - 1, span], dst_ref=arrived.at[step - 1, span],
            send_sem=peer_send.at[step - 1, span], recv_sem=peer_recv.at[step - 1, span],
            device_id=device(line, (row + step) % peers, core), device_id_type=pl.DeviceIdType.MESH)

    def table_copy(span):
        return pltpu.make_async_copy(tables_ref.at[0, span], table_buf.at[span], table_sem.at[span])

    barrier = pltpu.get_barrier_semaphore()

    def greet(target):
        pl.semaphore_signal(barrier, inc=1, device_id=target, device_id_type=pl.DeviceIdType.MESH)

    greet(device(line, row, sibling))
    for step in range(1, peers):
        greet(device(line, (row + step) % peers, core))

    @pl.when(line < lines - 1)
    def _():
        greet(device(line + 1, row, core))

    @pl.when(line > 0)
    def _():
        greet(device(line - 1, row, core))

    for span in range(spans):
        table_copy(span).start()

    block_ids = lax.broadcasted_iota(jnp.int32, (LANES, pairs_ref.shape[1]), 0)
    span_ids = lax.broadcasted_iota(jnp.int32, (8, pairs_ref.shape[1]), 0)
    block_match = jnp.where(block_ids == pairs_ref[0:1, :], 1.0, 0.0).astype(jnp.bfloat16)
    span_match = jnp.where(span_ids == pairs_ref[1:2, :], 1.0, 0.0).astype(jnp.bfloat16)
    needed = lax.dot_general(
        span_match, block_match, (((1,), (1,)), ((), ())), preferred_element_type=jnp.float32)
    last = rows - 16
    tail_rows = lax.broadcasted_iota(jnp.int32, (16, LANES), 0) + last
    for span in range(spans):
        raw[line, core, span, last:rows, :] = jnp.zeros((16, LANES), jnp.bfloat16)
        raw[line, core, span, 0:cols, :] = spectra_ref[0, span]
        tail = raw[line, core, span, last:rows, :].astype(jnp.float32)
        flags = jnp.broadcast_to(needed[span:span + 1, :], (16, LANES))
        raw[line, core, span, last:rows, :] = jnp.where(tail_rows < cols, tail, flags).astype(jnp.bfloat16)

    ends = jnp.where(line > 0, 1, 0) + jnp.where(line < lines - 1, 1, 0)
    pl.semaphore_wait(barrier, peers + ends)

    lane = lax.broadcasted_iota(jnp.int32, (8, LANES), 1)

    def mix(span):
        half = (rows // 32) * 16
        for start, size in ((0, half), (half, rows - half)):
            totals = [jnp.zeros((size // 8, 8, LANES), jnp.float32) for _ in range(peers)]
            for at_line in range(lines):
                for at_core in range(CORES):
                    values = raw[at_line, at_core, span, start:start + size, :].astype(jnp.float32)
                    values = values.reshape(size // 8, 8, LANES)
                    marks = raw[at_line, at_core, span, last:rows, :].astype(jnp.float32)[8:16]
                    for step in range(peers):
                        target = (line * peers + (row + step) % peers) * CORES + core
                        factor = jnp.sum(jnp.where(lane == target, marks, 0.0), axis=1, keepdims=True)
                        totals[step] = totals[step] + values * factor[None]
            own_sum[span, start:start + size, :] = totals[0].reshape(size, LANES)
            for step in range(1, peers):
                sums[step - 1, span, start:start + size, :] = totals[step].reshape(size, LANES)
        for step in range(1, peers):
            peer_copy(step, span).start()

    def multiply(span):
        total = own_sum[span]
        for step in range(1, peers):
            peer_copy(step, span).wait_recv()
            total = total + arrived[step - 1, span]
        high = total.astype(jnp.bfloat16)
        low = (total - high.astype(jnp.float32)).astype(jnp.bfloat16)
        factors[:, 0:LANES] = high
        factors[:, LANES:2 * LANES] = low
        table_copy(span).wait()

        def tile(index, carry):
            where = pl.ds(pl.multiple_of(index * TILE, TILE), TILE)
            block = table_buf[span, where, :]
            block = jnp.concatenate([block, block], axis=1)
            part = lax.dot_general(
                factors[...], block, (((1,), (1,)), ((), ())), preferred_element_type=jnp.float32)[:cols]
            if span == 0:
                out_ref[0, :, where] = part
            else:
                out_ref[0, :, where] += part
            return carry

        lax.fori_loop(0, out_ref.shape[2] // TILE, tile, 0)

    for tick in range(spans + lines):
        for dist in range(lines):
            span = tick - dist
            if not 0 <= span < spans:
                continue
            if dist == 0:
                @pl.when(line < lines - 1)
                def _():
                    up_copy(0, span).start()

                @pl.when(line > 0)
                def _():
                    down_copy(0, span).start()

                core_copy(line, span).start()
            else:
                @pl.when(line >= dist)
                def _():
                    up_copy(dist - 1, span).wait_recv()
                    if dist < lines - 1:
                        @pl.when(line < lines - 1)
                        def _():
                            up_copy(dist, span).start()
                    core_copy(line - dist, span).start()

                @pl.when(line + dist < lines)
                def _():
                    down_copy(dist - 1, span).wait_recv()
                    if dist < lines - 1:
                        @pl.when(line > 0)
                        def _():
                            down_copy(dist, span).start()
                    core_copy(line + dist, span).start()
        done = tick - (lines - 1)
        if 0 <= done < spans:
            for at_line in range(lines):
                core_copy(at_line, done).wait_recv()
            mix(done)
        if 0 <= done - 1 < spans:
            multiply(done - 1)

    for span in range(spans):
        for at_line in range(lines):
            core_copy(at_line, span).wait_send()
        for step in range(1, peers):
            peer_copy(step, span).wait_send()
        for dist in range(lines - 1):
            @pl.when(jnp.logical_and(line >= dist, line < lines - 1))
            def _():
                up_copy(dist, span).wait_send()

            @pl.when(jnp.logical_and(line + dist < lines, line > 0))
            def _():
                down_copy(dist, span).wait_send()


def local(owners, tables, spectra, pairs):
    lines, peers = chip_grid(owners)
    _, spans, size, depth = tables.shape
    cols = spectra.shape[2]
    rows = -(-(cols + 8) // 16) * 16
    dma = pltpu.SemaphoreType.DMA
    return pl.pallas_call(
        functools.partial(kernel, owners, lines, peers, cols),
        out_shape=jax.ShapeDtypeStruct((1, cols, size), jnp.float32),
        in_specs=[
            pl.BlockSpec(memory_space=pl.ANY),
            pl.BlockSpec(memory_space=pltpu.VMEM),
            pl.BlockSpec(memory_space=pltpu.VMEM),
        ],
        out_specs=pl.BlockSpec(memory_space=pltpu.VMEM),
        scratch_shapes=[
            pltpu.VMEM((lines, CORES, spans, rows, depth), jnp.bfloat16),
            pltpu.VMEM((spans, size, depth), jnp.bfloat16),
            pltpu.VMEM((peers - 1, spans, rows, depth), jnp.float32),
            pltpu.VMEM((peers - 1, spans, rows, depth), jnp.float32),
            pltpu.VMEM((rows, 2 * depth), jnp.bfloat16),
            pltpu.VMEM((spans, rows, depth), jnp.float32),
            dma((spans,)),
            dma((lines - 1, spans)),
            dma((lines - 1, spans)),
            dma((lines - 1, spans)),
            dma((lines - 1, spans)),
            dma((lines, spans)),
            dma((lines, spans)),
            dma((peers - 1, spans)),
            dma((peers - 1, spans)),
        ],
        compiler_params=pltpu.CompilerParams(
            collective_id=0, has_side_effects=True, vmem_limit_bytes=40 * 1024 * 1024
        ),
    )(tables, spectra, pairs.T)


def solution(mesh):
    owners = mesh.shape["lblk"]
    return jax.shard_map(
        functools.partial(local, owners),
        mesh=mesh,
        in_specs=(
            P("lblk", None, None, None),
            P(("groups", "lblk"), None, None, None),
            P(("groups", "lblk"), None),
        ),
        out_specs=P(("groups", "lblk"), None, None),
        check_vma=False,
    )
```

time: 79.7 us -> 42.5 us (0.53)
  Pallas kernels: 0 us -> 31.8 us
  waiting for transfers between devices: 25 us -> 0 us
  blocking collectives: 23.1 us -> 0 us
  between operations: 13.4 us -> 0.02 us
  matrix products: 11 us -> 0 us
  local copies, waits for them, and re-layouts: 7.09 us -> 10.5 us
    pallas_call x0 -> x1, Pallas kernels: none -> 31.8 us  [local(): pl.pallas_call(functools.partial(kernel, owners, lines, peers, cols), out...]
    all_gather x1 -> x0, waiting for transfers between devices: 24.3 us -> none  [local(): reader_part = lax.all_gather(spectra, 'lblk', axis=0, tiled=True)]
    all_gather x1 -> x0, blocking collectives: 23.1 us -> none  [local(): reader_flags = lax.all_gather(flags, 'lblk', axis=0, tiled=True)]
    dot_general x3 -> x0, matrix products: 11 us -> none  [the longest x1 8.48 us: local(): jnp.einsum('cjk,cik->ji', mixed, tables[0].astype(jnp.float32), precision...]
    broadcast_in_dim x1 -> x0, local copies, waits for them, and re-layouts: 6.13 us -> none  [local(): jnp.einsum('cjk,cik->ji', mixed, tables[0].astype(jnp.float32), precision...]
    pallas_call x0 -> x1, local copies, waits for them, and re-layouts: none -> 6.13 us  [local(): pl.pallas_call(functools.partial(kernel, owners, lines, peers, cols), out...]
    unnamed x0 -> x5, local copies, waits for them, and re-layouts: none -> 4.4 us
  transfers between devices with their start and end apart: 1 -> 0, of which waited for: 1 -> 0; matrix products, arithmetic and copies ran while one was open for 2% -> 0% of each run, Pallas kernels for 0% -> 0%
where the time goes in v1:
time: 42.5 us; the launch traced here: 42.3 us
  Pallas kernels  31.8 us (75%)
  local copies, waits for them, and re-layouts  10.5 us (25%)
    pallas_call x1, Pallas kernels, local(): pl.pallas_call(functools.partial(kernel, owners, lines, peers, cols), out...  31.8 us
    pallas_call x1, local copies, waits for them, and re-layouts, local(): pl.pallas_call(functools.partial(kernel, owners, lines, peers, cols), out...  6.13 us
    unnamed x5, local copies, waits for them, and re-layouts  4.4 us

profile of v1, /device:TPU:0, one launch (start us, length us, event | category | flops | bytes accessed | tf_op | source)
XLA Modules:
  0.0 42.3 jit_solution(6296951839611406755)
XLA Ops:
  0.0 0.9 %copy.4.spectra_ref = bf16[1,4,165,128]{3,2,1,0:T(8,128)(2,1)S(1)} copy(bf16[1,4,165,128]{3,1,2,0:T(4,128)(2,1)} %param.4) | data formatting | bytes 337920 | tf_op args[1]
  0.9 0.0 copy-start
  1.0 2.8 %copy-done = bf16[1,4,6144,128]{3,2,1,0:T(8,128)(2,1)S(1)} copy-done((bf16[1,4,6144,128]{3,2,1,0:T(8,128)(2,1)S(1)}, bf16[1,4,6144,128]{3,2,1,0:T(8,128)(2,1)}, u32[]{:S(2)}) %copy-start) | copy-done | bytes 6291480
  3.7 0.0 copy-start.1
  3.7 0.7 %copy-done.1 = s32[32,2]{0,1:T(2,128)S(1)} copy-done((s32[32,2]{0,1:T(2,128)S(1)}, s32[32,2]{0,1:T(2,128)}, u32[]{:S(2)}) %copy-start.1) | copy-done | bytes 280
  4.4 31.8 %shard_map.37 = f32[1,165,6144]{2,1,0:T(8,128)S(1)} custom-call(bf16[1,4,6144,128]{3,2,1,0:T(8,128)(2,1)S(1)} %copy-done, bf16[1,4,165,128]{3,2,1,0:T(8,128)(2,1)S(1)} %copy.4.spectra_ref, s32[2,32]{1,0:T(2,128)S(1)} %bitcast.1), custom_call_target="tpu_custom_call" | custom-call | tf_op jit(solution)/shard_map/pallas_call | solution.py:213
  36.2 6.1 %copy.5 = f32[1,165,6144]{2,0,1:T(1,128)} copy(f32[1,165,6144]{2,1,0:T(8,128)S(1)} %shard_map.37) | data formatting | bytes 8110080 | tf_op jit(solution)/shard_map/pallas_call | solution.py:213
Async XLA Ops:
  0.9 2.8 %copy-start = (bf16[1,4,6144,128]{3,2,1,0:T(8,128)(2,1)S(1)}, bf16[1,4,6144,128]{3,2,1,0:T(8,128)(2,1)}, u32[]{:S(2)}) copy-start(bf16[1,4,6144,128]{3,2,1,0:T(8,128)(2,1)} %tables_ref.1) | copy-start | bytes 18874372
  3.7 0.7 %copy-start.1 = (s32[32,2]{0,1:T(2,128)S(1)}, s32[32,2]{0,1:T(2,128)}, u32[]{:S(2)}) copy-start(s32[32,2]{0,1:T(2,128)} %param.5) | copy-start | bytes 772

commit v2 on v1

v2 whole, which is shorter than its diff:
```python
import functools

import jax
import jax.numpy as jnp
from jax import lax
from jax.experimental import pallas as pl
from jax.experimental.pallas import tpu as pltpu
from jax.sharding import PartitionSpec as P

LANES = 128
CORES = 2
TILE = 1024
DIRECT = 1


def cut_spans(spans):
    pieces, start, size = [], 0, max(spans // 2, 1)
    while start < spans:
        pieces.append((start, size))
        start += size
    return pieces


def chip_grid(owners):
    chips = owners // CORES
    inner = 1
    while (inner * 2) ** 2 <= chips:
        inner *= 2
    return chips // inner, inner


def kernel(
    lines, peers, cols, pieces,
    tables_ref, spectra_ref, pairs_ref, out_ref,
    raw, table_buf, sums, arrived, factors, own_sum, product, own_rows, own_wide, list_buf,
    table_sem, own_sem, list_sem, line_send, line_recv, core_send, core_recv, peer_send, peer_recv,
):
    spans = tables_ref.shape[1]
    rows = raw.shape[3]
    me = lax.axis_index("lblk")
    line = me // (peers * CORES)
    row = (me // CORES) % peers
    core = me % CORES
    sibling = 1 - core

    def device(at_line, at_row, at_core):
        return {"lblk": (at_line * peers + at_row) * CORES + at_core}

    def line_copy(way, dist, piece):
        hop = dist if dist <= DIRECT else 1
        unit = jnp.clip(line - way * (dist - hop), 0, lines - 1)
        target = jnp.clip(line + way * hop, 0, lines - 1)
        start, size = pieces[piece]
        slot = raw.at[unit, core, pl.ds(start, size)]
        side = 0 if way > 0 else 1
        return pltpu.make_async_remote_copy(
            src_ref=slot, dst_ref=slot, send_sem=line_send.at[side, dist - 1, piece],
            recv_sem=line_recv.at[side, dist - 1, piece],
            device_id=device(target, row, core), device_id_type=pl.DeviceIdType.MESH)

    def inside(at_line):
        return jnp.logical_and(at_line >= 0, at_line < lines)

    def sends(way, dist):
        hop = dist if dist <= DIRECT else 1
        return jnp.logical_and(inside(line + way * hop), inside(line - way * (dist - hop)))

    def core_copy(at_line, piece):
        start, size = pieces[piece]
        slot = raw.at[at_line, core, pl.ds(start, size)]
        return pltpu.make_async_remote_copy(
            src_ref=slot, dst_ref=slot, send_sem=core_send.at[at_line, piece], recv_sem=core_recv.at[at_line, piece],
            device_id=device(line, row, sibling), device_id_type=pl.DeviceIdType.MESH)

    def peer_copy(step, piece):
        start, size = pieces[piece]
        return pltpu.make_async_remote_copy(
            src_ref=sums.at[step - 1, pl.ds(start, size)], dst_ref=arrived.at[step - 1, pl.ds(start, size)],
            send_sem=peer_send.at[step - 1, piece], recv_sem=peer_recv.at[step - 1, piece],
            device_id=device(line, (row + step) % peers, core), device_id_type=pl.DeviceIdType.MESH)

    def table_copy(span):
        return pltpu.make_async_copy(tables_ref.at[0, span], table_buf.at[span], table_sem.at[span])

    barrier = pltpu.get_barrier_semaphore()

    def greet(target):
        pl.semaphore_signal(barrier, inc=1, device_id=target, device_id_type=pl.DeviceIdType.MESH)

    greet(device(line, row, sibling))
    for step in range(1, peers):
        greet(device(line, (row + step) % peers, core))

    neighbours = jnp.int32(peers)
    for hop in range(1, min(DIRECT, lines - 1) + 1):
        for way in (1, -1):
            there = inside(line + way * hop)
            neighbours = neighbours + jnp.where(there, 1, 0)

            @pl.when(there)
            def _():
                greet(device(line + way * hop, row, core))

    own_copy = pltpu.make_async_copy(spectra_ref, own_rows, own_sem)
    list_copy = pltpu.make_async_copy(pairs_ref, list_buf, list_sem)
    list_copy.start()
    own_copy.start()
    for span in range(spans):
        table_copy(span).start()

    list_copy.wait()
    block_ids = lax.broadcasted_iota(jnp.int32, (LANES, pairs_ref.shape[1]), 0)
    span_ids = lax.broadcasted_iota(jnp.int32, (8, pairs_ref.shape[1]), 0)
    block_match = jnp.where(block_ids == list_buf[0:1, :], 1.0, 0.0).astype(jnp.bfloat16)
    span_match = jnp.where(span_ids == list_buf[1:2, :], 1.0, 0.0).astype(jnp.bfloat16)
    needed = lax.dot_general(
        span_match, block_match, (((1,), (1,)), ((), ())), preferred_element_type=jnp.float32)
    own_copy.wait()
    own_wide[...] = own_rows[0].astype(jnp.float32).reshape(cols * spans, LANES)
    last = rows - 16
    tail_rows = lax.broadcasted_iota(jnp.int32, (16, LANES), 0) + last
    for span in range(spans):
        raw[line, core, span, last:rows, :] = jnp.zeros((16, LANES), jnp.bfloat16)
        raw[line, core, span, 0:cols, :] = own_wide[pl.ds(span, cols, stride=spans), :].astype(jnp.bfloat16)
        tail = raw[line, core, span, last:rows, :].astype(jnp.float32)
        flags = jnp.broadcast_to(needed[span:span + 1, :], (16, LANES))
        raw[line, core, span, last:rows, :] = jnp.where(tail_rows < cols, tail, flags).astype(jnp.bfloat16)

    pl.semaphore_wait(barrier, neighbours)

    for piece in range(len(pieces)):
        for dist in range(min(DIRECT, lines - 1), 0, -1):
            for way in (1, -1):
                @pl.when(sends(way, dist))
                def _():
                    line_copy(way, dist, piece).start()
        core_copy(line, piece).start()

    lane = lax.broadcasted_iota(jnp.int32, (8, LANES), 1)

    def mix(span):
        half = (rows // 32) * 16
        for start, size in ((0, half), (half, rows - half)):
            totals = [jnp.zeros((size // 8, 8, LANES), jnp.float32) for _ in range(peers)]
            for at_line in range(lines):
                for at_core in range(CORES):
                    values = raw[at_line, at_core, span, start:start + size, :].astype(jnp.float32)
                    values = values.reshape(size // 8, 8, LANES)
                    marks = raw[at_line, at_core, span, last:rows, :].astype(jnp.float32)[8:16]
                    for step in range(peers):
                        target = (line * peers + (row + step) % peers) * CORES + core
                        factor = jnp.sum(jnp.where(lane == target, marks, 0.0), axis=1, keepdims=True)
                        totals[step] = totals[step] + values * factor[None]
            own_sum[span, start:start + size, :] = totals[0].reshape(size, LANES)
            for step in range(1, peers):
                sums[step - 1, span, start:start + size, :] = totals[step].reshape(size, LANES)

    def multiply(piece):
        first, count = pieces[piece]
        for step in range(1, peers):
            peer_copy(step, piece).wait_recv()
        for at in range(count):
            total = own_sum[first + at]
            for step in range(1, peers):
                total = total + arrived[step - 1, first + at]
            high = total.astype(jnp.bfloat16)
            low = (total - high.astype(jnp.float32)).astype(jnp.bfloat16)
            factors[:, 2 * at * LANES:(2 * at + 1) * LANES] = high
            factors[:, (2 * at + 1) * LANES:(2 * at + 2) * LANES] = low
            table_copy(first + at).wait()

        def tile(index, carry):
            where = pl.ds(pl.multiple_of(index * TILE, TILE), TILE)
            blocks = [table_buf[first + at, where, :] for at in range(count)]
            block = jnp.concatenate([blocks[at // 2] for at in range(2 * count)], axis=1)
            part = lax.dot_general(
                factors[:, 0:2 * count * LANES], block, (((1,), (1,)), ((), ())), preferred_element_type=jnp.float32)[:cols]
            if first == 0:
                product[:, where] = part
            elif first + count < spans:
                product[:, where] += part
            else:
                out_ref[:, 0, where] = product[:, where] + part
            return carry

        lax.fori_loop(0, out_ref.shape[2] // TILE, tile, 0)

    events = sorted(
        ((dist, piece) for dist in range(1, lines) for piece in range(len(pieces))),
        key=lambda event: (event[0] + event[1], event[0]))
    for dist, piece in events:
        for way in (1, -1):
            @pl.when(inside(line - way * dist))
            def _():
                line_copy(way, dist, piece).wait_recv()
                if DIRECT <= dist < lines - 1:
                    @pl.when(sends(way, dist + 1))
                    def _():
                        line_copy(way, dist + 1, piece).start()
                core_copy(line - way * dist, piece).start()
        if dist < lines - 1:
            continue
        for at_line in range(lines):
            core_copy(at_line, piece).wait_recv()
        first, count = pieces[piece]
        for at in range(count):
            mix(first + at)
        for step in range(1, peers):
            peer_copy(step, piece).start()
        if piece > 0:
            multiply(piece - 1)
    multiply(len(pieces) - 1)

    for piece in range(len(pieces)):
        for at_line in range(lines):
            core_copy(at_line, piece).wait_send()
        for step in range(1, peers):
            peer_copy(step, piece).wait_send()
        for dist in range(1, lines):
            for way in (1, -1):
                @pl.when(sends(way, dist))
                def _():
                    line_copy(way, dist, piece).wait_send()


def local(owners, tables, spectra, pairs):
    lines, peers = chip_grid(owners)
    _, spans, size, depth = tables.shape
    cols = spectra.shape[2]
    pieces = cut_spans(spans)
    rows = -(-(cols + 8) // 16) * 16
    dma = pltpu.SemaphoreType.DMA
    result = pl.pallas_call(
        functools.partial(kernel, lines, peers, cols, pieces),
        out_shape=jax.ShapeDtypeStruct((cols, 1, size), jnp.float32),
        in_specs=[
            pl.BlockSpec(memory_space=pltpu.HBM),
            pl.BlockSpec(memory_space=pltpu.HBM),
            pl.BlockSpec(memory_space=pltpu.HBM),
        ],
        out_specs=pl.BlockSpec(memory_space=pltpu.VMEM),
        scratch_shapes=[
            pltpu.VMEM((lines, CORES, spans, rows, depth), jnp.bfloat16),
            pltpu.VMEM((spans, size, depth), jnp.bfloat16),
            pltpu.VMEM((peers - 1, spans, rows, depth), jnp.float32),
            pltpu.VMEM((peers - 1, spans, rows, depth), jnp.float32),
            pltpu.VMEM((rows, 2 * depth * max(count for _, count in pieces)), jnp.bfloat16),
            pltpu.VMEM((spans, rows, depth), jnp.float32),
            pltpu.VMEM((cols, size), jnp.float32),
            pltpu.VMEM((1, cols, spans, depth), jnp.bfloat16),
            pltpu.VMEM((cols * spans, depth), jnp.float32),
            pltpu.VMEM((2, pairs.shape[0]), jnp.int32),
            dma((spans,)),
            dma(()),
            dma(()),
            dma((2, lines - 1, len(pieces))),
            dma((2, lines - 1, len(pieces))),
            dma((lines, len(pieces))),
            dma((lines, len(pieces))),
            dma((peers - 1, len(pieces))),
            dma((peers - 1, len(pieces))),
        ],
        compiler_params=pltpu.CompilerParams(
            collective_id=0, has_side_effects=True, vmem_limit_bytes=52000000
        ),
    )(tables, spectra.transpose(0, 2, 1, 3), pairs.T)
    return result.transpose(1, 0, 2)


def solution(mesh):
    owners = mesh.shape["lblk"]
    return jax.shard_map(
        functools.partial(local, owners),
        mesh=mesh,
        in_specs=(
            P("lblk", None, None, None),
            P(("groups", "lblk"), None, None, None),
            P(("groups", "lblk"), None),
        ),
        out_specs=P(("groups", "lblk"), None, None),
        check_vma=False,
    )
```

time: 42.5 us -> 34.5 us (0.81)
  local copies, waits for them, and re-layouts: 10.5 us -> 3.56 us
  Pallas kernels: 31.8 us -> 30.8 us
    pallas_call x1 -> x0, local copies, waits for them, and re-layouts: 6.13 us -> none  [local(): pl.pallas_call(functools.partial(kernel, owners, lines, peers, cols), out...]
    pallas_call x1, Pallas kernels: 31.8 us -> 30.8 us  [local(): pl.pallas_call(functools.partial(kernel, lines, peers, cols, pieces), out...]
    unnamed x5, local copies, waits for them, and re-layouts: 4.4 us -> 3.56 us
where the time goes in v2:
time: 34.5 us; the launch traced here: 34.3 us
  Pallas kernels  30.8 us (89%)
  local copies, waits for them, and re-layouts  3.56 us (10%)
    pallas_call x1, Pallas kernels, local(): pl.pallas_call(functools.partial(kernel, lines, peers, cols, pieces), out...  30.8 us
    unnamed x5, local copies, waits for them, and re-layouts  3.56 us

profile of v2, /device:TPU:0, one launch (start us, length us, event | category | flops | bytes accessed | tf_op | source)
XLA Modules:
  0.0 34.3 jit_solution(17987203339755199807)
XLA Ops:
  0.0 0.0 copy-start
  0.0 0.9 %copy-done = bf16[1,4,165,128]{3,1,2,0:T(4,128)(2,1)S(1)} copy-done((bf16[1,4,165,128]{3,1,2,0:T(4,128)(2,1)S(1)}, bf16[1,4,165,128]{3,1,2,0:T(4,128)(2,1)}, u32[]{:S(2)}) %copy-start) | copy-done | bytes 168984
  0.9 0.0 copy-start.1
  0.9 0.7 %copy-done.1 = s32[32,2]{0,1:T(2,128)S(1)} copy-done((s32[32,2]{0,1:T(2,128)S(1)}, s32[32,2]{0,1:T(2,128)}, u32[]{:S(2)}) %copy-start.1) | copy-done | bytes 280
  1.6 30.8 %shard_map.37 = f32[165,1,6144]{2,1,0:T(1,128)S(1)} custom-call(bf16[1,4,6144,128]{3,2,1,0:T(8,128)(2,1)} %tables_ref.1, bf16[1,165,4,128]{3,2,1,0:T(4,128)(2,1)S(1)} %bitcast.4, s32[2,32]{1,0:T(2,128)S(1)} %bitcast.5), custom_call_target="tpu_custom_call" | custom-call | tf_op jit(solution)/shard_map/pallas_call | solution.py:233
  32.4 2.0 %copy.5 = f32[1,165,6144]{2,0,1:T(1,128)} copy(f32[1,165,6144]{2,0,1:T(1,128)S(1)} %bitcast.3) | data formatting | bytes 8110080
Async XLA Ops:
  0.0 0.9 %copy-start = (bf16[1,4,165,128]{3,1,2,0:T(4,128)(2,1)S(1)}, bf16[1,4,165,128]{3,1,2,0:T(4,128)(2,1)}, u32[]{:S(2)}) copy-start(bf16[1,4,165,128]{3,1,2,0:T(4,128)(2,1)} %param.4) | copy-start | bytes 506884
  0.9 0.7 %copy-start.1 = (s32[32,2]{0,1:T(2,128)S(1)}, s32[32,2]{0,1:T(2,128)}, u32[]{:S(2)}) copy-start(s32[32,2]{0,1:T(2,128)} %param.5) | copy-start | bytes 772

commit v3 on v2

--- a/solution.py
+++ b/solution.py
@@ -9,7 +9,7 @@
 
 LANES = 128
 CORES = 2
-TILE = 1024
+TILE = 3072
 DIRECT = 1
 
 

time: 34.5 us -> 33.8 us (0.980)
  Pallas kernels: 30.8 us -> 30.1 us
    pallas_call x1, Pallas kernels: 30.8 us -> 30.1 us  [local(): pl.pallas_call(functools.partial(kernel, lines, peers, cols, pieces), out...]
where the time goes in v3:
time: 33.8 us; the launch traced here: 33.7 us
  Pallas kernels  30.1 us (89%)
  local copies, waits for them, and re-layouts  3.56 us (11%)
    pallas_call x1, Pallas kernels, local(): pl.pallas_call(functools.partial(kernel, lines, peers, cols, pieces), out...  30.1 us
    unnamed x5, local copies, waits for them, and re-layouts  3.56 us

profile of v3, /device:TPU:0, one launch (start us, length us, event | category | flops | bytes accessed | tf_op | source)
XLA Modules:
  0.0 33.7 jit_solution(5945747810087177276)
XLA Ops:
  0.0 0.0 copy-start
  0.0 0.9 %copy-done = bf16[1,4,165,128]{3,1,2,0:T(4,128)(2,1)S(1)} copy-done((bf16[1,4,165,128]{3,1,2,0:T(4,128)(2,1)S(1)}, bf16[1,4,165,128]{3,1,2,0:T(4,128)(2,1)}, u32[]{:S(2)}) %copy-start) | copy-done | bytes 168984
  0.9 0.0 copy-start.1
  0.9 0.7 %copy-done.1 = s32[32,2]{0,1:T(2,128)S(1)} copy-done((s32[32,2]{0,1:T(2,128)S(1)}, s32[32,2]{0,1:T(2,128)}, u32[]{:S(2)}) %copy-start.1) | copy-done | bytes 280
  1.6 30.1 %shard_map.37 = f32[165,1,6144]{2,1,0:T(1,128)S(1)} custom-call(bf16[1,4,6144,128]{3,2,1,0:T(8,128)(2,1)} %tables_ref.1, bf16[1,165,4,128]{3,2,1,0:T(4,128)(2,1)S(1)} %bitcast.4, s32[2,32]{1,0:T(2,128)S(1)} %bitcast.5), custom_call_target="tpu_custom_call" | custom-call | tf_op jit(solution)/shard_map/pallas_call | solution.py:233
  31.7 2.0 %copy.5 = f32[1,165,6144]{2,0,1:T(1,128)} copy(f32[1,165,6144]{2,0,1:T(1,128)S(1)} %bitcast.3) | data formatting | bytes 8110080
Async XLA Ops:
  0.0 0.9 %copy-start = (bf16[1,4,165,128]{3,1,2,0:T(4,128)(2,1)S(1)}, bf16[1,4,165,128]{3,1,2,0:T(4,128)(2,1)}, u32[]{:S(2)}) copy-start(bf16[1,4,165,128]{3,1,2,0:T(4,128)(2,1)} %param.4) | copy-start | bytes 506884
  0.9 0.7 %copy-start.1 = (s32[32,2]{0,1:T(2,128)S(1)}, s32[32,2]{0,1:T(2,128)}, u32[]{:S(2)}) copy-start(s32[32,2]{0,1:T(2,128)} %param.5) | copy-start | bytes 772
